TPU v7x, 32 devices: a whole 2x2x4 slice. The times are simulated.
32 devices in a mesh: groups: 2 (over x), gx: 4 (over y, core), gy: 4 (over z).
Axes of the slice: x: 2, y: 2, z: 4, core: 2. Of those that a mesh axis runs over, the one named last changes fastest.
Arguments:
- inputs: bfloat16 [32, 16, 58, 128], P(('groups', 'gx'), 'gy'), parts along dimension 0, may hold values from -6 to 6
- target: bfloat16 [32, 16, 53, 128], P(('groups', 'gx'), 'gy'), parts along dimension 0, may hold values from -6 to 6
- w_first: bfloat16 [3, 3, 3, 58, 64], replicated, may hold values from -0.15625 to 0.15625
- w_second: bfloat16 [3, 3, 3, 64, 53], replicated, may hold values from -0.15625 to 0.15625
Outputs:
- prediction: bfloat16 [32, 16, 53, 128], P(('groups', 'gx'), 'gy'), parts along dimension 0
- grad_first: float32 [6, 3, 3, 58, 64], P('groups'), parts along dimension 0
- grad_second: float32 [6, 3, 3, 64, 53], P('groups'), parts along dimension 0
There are 2 independent parts, one for each index of `groups`. A program takes and returns all parts, laid end to end along the dimension named above; an argument that names none is the same for every part. Nothing has to cross between parts.
All inputs are finite; a program needn't handle non-finite values.
Results may differ from a plain program's by a relative error of at most 0.0049.
Values may be sent and summed in bfloat16 or wider, within the bound.
A program may use at most 64 MiB of HBM per device.

v0:
```python
import math
import jax
import jax.numpy as jnp
from jax import lax
from jax.sharding import PartitionSpec as P

root_two_pi = 0.7978845608028654
cubic_term = 0.044715


def extended(cells, sides, width):
    for axis, dim in sides:
        count = lax.axis_size(axis)
        ends = count - 1
        head = lax.slice_in_dim(cells, 0, width, axis=dim)
        tail = lax.slice_in_dim(cells, cells.shape[dim] - width, cells.shape[dim], axis=dim)
        cells = jnp.concatenate(
            [
                lax.ppermute(tail, axis, [(i, (i + 1) % count) for i in range(ends)]),
                cells,
                lax.ppermute(head, axis, [((i + 1) % count, i) for i in range(ends)]),
            ],
            axis=dim,
        )
    return cells


def shifted(value, axis, steps):
    count = lax.axis_size(axis)
    leading, last = (max(0, -steps), min(count, count - steps))
    return lax.ppermute(value, axis, [(source, source + steps) for source in range(leading, last)])


def smooth_gate(activation):
    tangent = jnp.tanh(
        root_two_pi * (activation + cubic_term * activation * activation * activation)
    )
    return 0.5 * activation * (1.0 + tangent)


def gate_slope(activation):
    tangent = jnp.tanh(
        root_two_pi * (activation + cubic_term * activation * activation * activation)
    )
    return 0.5 * (1.0 + tangent) + 0.5 * activation * (1.0 - tangent * tangent) * root_two_pi * (
        1.0 + 3.0 * cubic_term * activation * activation
    )


def depth_padded(field):
    return jnp.pad(field, ((0, 0), (0, 0), (0, 0), (1, 1)))


def correlate(field, kernel):
    extent_x = field.shape[0] - 2
    extent_y = field.shape[1] - 2
    depth = field.shape[3]
    padded = depth_padded(field)
    total = jnp.zeros((extent_x, extent_y, kernel.shape[4], depth), jnp.float32)
    for step_a in range(3):
        for step_b in range(3):
            for step_c in range(3):
                window = padded[
                    step_a : step_a + extent_x,
                    step_b : step_b + extent_y,
                    :,
                    step_c : step_c + depth,
                ]
                total = total + jnp.einsum(
                    "xycz,co->xyoz",
                    window,
                    kernel[step_a, step_b, step_c],
                    preferred_element_type=jnp.float32,
                )
    return total


def correlate_back(field, kernel):
    extent_x = field.shape[0] - 2
    extent_y = field.shape[1] - 2
    depth = field.shape[3]
    padded = depth_padded(field)
    total = jnp.zeros((extent_x, extent_y, kernel.shape[3], depth), jnp.float32)
    for step_a in range(3):
        for step_b in range(3):
            for step_c in range(3):
                window = padded[
                    2 - step_a : 2 - step_a + extent_x,
                    2 - step_b : 2 - step_b + extent_y,
                    :,
                    2 - step_c : 2 - step_c + depth,
                ]
                total = total + jnp.einsum(
                    "xyoz,io->xyiz",
                    window,
                    kernel[step_a, step_b, step_c],
                    preferred_element_type=jnp.float32,
                )
    return total


def filter_grad(field, slope_term):
    extent_x = slope_term.shape[0]
    extent_y = slope_term.shape[1]
    depth = slope_term.shape[3]
    padded = depth_padded(field)
    planes = []
    for step_a in range(3):
        rows_b = []
        for step_b in range(3):
            rows_c = []
            for step_c in range(3):
                window = padded[
                    step_a : step_a + extent_x,
                    step_b : step_b + extent_y,
                    :,
                    step_c : step_c + depth,
                ]
                rows_c.append(
                    jnp.einsum(
                        "xycz,xyoz->co", window, slope_term, preferred_element_type=jnp.float32
                    )
                )
            rows_b.append(jnp.stack(rows_c))
        planes.append(jnp.stack(rows_b))
    return jnp.stack(planes)


def on_device(inputs, target, w_first, w_second):
    block_x = inputs.shape[0]
    block_y = inputs.shape[1]
    padded_in = extended(inputs, (("gx", 0), ("gy", 1)), 1)
    activation = correlate(padded_in, w_first)
    hidden = smooth_gate(activation).astype(jnp.bfloat16)
    padded_hidden = extended(hidden, (("gx", 0), ("gy", 1)), 1)
    output = correlate(padded_hidden, w_second)
    prediction = output.astype(jnp.bfloat16)
    cell_count = block_x * lax.axis_size("gx") * block_y * lax.axis_size("gy") * inputs.shape[3]
    normalizer = 1.0 / math.sqrt(cell_count)
    output_grad = ((output - target.astype(jnp.float32)) * normalizer).astype(jnp.bfloat16)
    grad_second = filter_grad(padded_hidden, output_grad)
    widened = jnp.pad(output_grad, ((2, 2), (2, 2), (0, 0), (0, 0)))
    spread = correlate_back(widened, w_second)
    extent_x = spread.shape[0]
    from_below = shifted(spread[extent_x - 1 :].astype(jnp.bfloat16), "gx", 1).astype(jnp.float32)
    from_above = shifted(spread[:1].astype(jnp.bfloat16), "gx", -1).astype(jnp.float32)
    summed_x = spread[1 : extent_x - 1]
    summed_x = summed_x.at[:1].add(from_below).at[-1:].add(from_above)
    extent_y = summed_x.shape[1]
    from_left = shifted(summed_x[:, extent_y - 1 :].astype(jnp.bfloat16), "gy", 1).astype(
        jnp.float32
    )
    from_right = shifted(summed_x[:, :1].astype(jnp.bfloat16), "gy", -1).astype(jnp.float32)
    back_grad = summed_x[:, 1 : extent_y - 1].at[:, :1].add(from_left).at[:, -1:].add(from_right)
    slope_term = (back_grad * gate_slope(activation)).astype(jnp.bfloat16)
    grad_first = filter_grad(padded_in, slope_term)
    grad_first, grad_second = lax.psum((grad_first, grad_second), ("gx", "gy"))
    return (prediction, grad_first, grad_second)


def solution(mesh):
    placed = (
        P(("groups", "gx"), "gy", None, None),
        P(("groups", "gx"), "gy", None, None),
        P(),
        P(),
    )
    return jax.shard_map(
        on_device,
        mesh=mesh,
        in_specs=placed,
        out_specs=(
            P(("groups", "gx"), "gy", None, None),
            P("groups", None, None, None, None),
            P("groups", None, None, None, None),
        ),
        check_vma=False,
    )
```

profile of v0, /device:TPU:0, one launch (start us, length us, event | category | flops | bytes accessed | tf_op | source)
XLA Modules:
  0.0 207.4 jit_solution(16586595825704326842)
XLA Ops:
  7.2 0.9 fusion.357
  8.2 2.4 %collective-permute-start = (bf16[1,4,58,128]{3,2,1,0:T(8,128)(2,1)S(1)}, bf16[1,4,58,128]{3,2,1,0:T(8,128)(2,1)S(1)}, u32[]{:S(2)}, u32[]{:S(2)}) collective-permute-start(bf16[1,4,58,128]{3,2,1,0:T(8,128)(2,1)S(1)} %copy.188), channel_id=1, source_target_pairs={{0,4},{4,8},{8,12},{1,5},{5,9},{9,13},{2,6},{6,10},{10,14},{3,7},{... | collective-permute-start | bytes 178184 | tf_op jit(solution)/shard_map/ppermute | solution.py:19
  10.6 1.3 collective-permute-start.1
  11.9 1.2 constant_dynamic-update-slice_fusion.6
  13.1 2.8 %collective-permute-done.1 = bf16[1,4,58,128]{3,2,1,0:T(8,128)(2,1)S(1)} collective-permute-done((bf16[1,4,58,128]{3,2,1,0:T(8,128)(2,1)S(1)}, bf16[1,4,58,128]{3,2,1,0:T(8,128)(2,1)S(1)}, u32[]{:S(2)}, u32[]{:S(2)}) %collective-permute-start.1) | collective-permute-done | bytes 59424 | tf_op jit(solution)/shard_map/ppermute | solution.py:21
  15.9 3.5 %collective-permute-start.2 = (bf16[6,1,58,128]{3,2,1,0:T(8,128)(2,1)S(1)}, bf16[6,1,58,128]{3,2,1,0:T(8,128)(2,1)S(1)}, u32[]{:S(2)}, u32[]{:S(2)}) collective-permute-start(bf16[6,1,58,128]{3,2,1,0:T(8,128)(2,1)S(1)} %get-tuple-element.64), channel_id=1, source_target_pairs={{0,1},{1,2},{2,3},{4,5},{5,6},{6,7},{8,9},{9,10},{10,11},{12,13},{... | collective-permute-start | bytes 267272 | tf_op jit(solution)/shard_map/ppermute | solution.py:19
  19.4 1.3 collective-permute-start.3
  21.0 0.6 collective-permute-done.2
  21.6 4.3 %collective-permute-done.3 = bf16[6,1,58,128]{3,2,1,0:T(8,128)(2,1)S(1)} collective-permute-done((bf16[6,1,58,128]{3,2,1,0:T(8,128)(2,1)S(1)}, bf16[6,1,58,128]{3,2,1,0:T(8,128)(2,1)S(1)}, u32[]{:S(2)}, u32[]{:S(2)}) %collective-permute-start.3) | collective-permute-done | bytes 89120 | tf_op jit(solution)/shard_map/ppermute | solution.py:21
  25.9 0.6 fusion.57
  32.0 0.7 copy-done
  35.2 3.4 %collective-permute-start.4 = (bf16[1,4,64,128]{3,2,1,0:T(8,128)(2,1)S(1)}, bf16[1,4,64,128]{3,2,1,0:T(8,128)(2,1)S(1)}, u32[]{:S(2)}, u32[]{:S(2)}) collective-permute-start(bf16[1,4,64,128]{3,2,1,0:T(8,128)(2,1)S(1)} %get-tuple-element.66), channel_id=1, source_target_pairs={{0,4},{4,8},{8,12},{1,5},{5,9},{9,13},{2,6},{6,10},{10,14},{3,7},{... | collective-permute-start | bytes 196616 | tf_op jit(solution)/shard_map/ppermute | solution.py:19
  38.6 1.4 collective-permute-start.5
  40.0 2.7 %collective-permute-done.5 = bf16[1,4,64,128]{3,2,1,0:T(8,128)(2,1)S(1)} collective-permute-done((bf16[1,4,64,128]{3,2,1,0:T(8,128)(2,1)S(1)}, bf16[1,4,64,128]{3,2,1,0:T(8,128)(2,1)S(1)}, u32[]{:S(2)}, u32[]{:S(2)}) %collective-permute-start.5) | collective-permute-done | bytes 65568 | tf_op jit(solution)/shard_map/ppermute | solution.py:21
  42.8 3.5 %collective-permute-start.6 = (bf16[6,1,64,128]{3,2,1,0:T(8,128)(2,1)S(1)}, bf16[6,1,64,128]{3,2,1,0:T(8,128)(2,1)S(1)}, u32[]{:S(2)}, u32[]{:S(2)}) collective-permute-start(bf16[6,1,64,128]{3,2,1,0:T(8,128)(2,1)S(1)} %get-tuple-element.62), channel_id=1, source_target_pairs={{0,1},{1,2},{2,3},{4,5},{5,6},{6,7},{8,9},{9,10},{10,11},{12,13},{... | collective-permute-start | bytes 294920 | tf_op jit(solution)/shard_map/ppermute | solution.py:19
  46.3 1.5 collective-permute-start.7
  47.8 0.7 collective-permute-done.6
  48.5 4.3 %collective-permute-done.7 = bf16[6,1,64,128]{3,2,1,0:T(8,128)(2,1)S(1)} collective-permute-done((bf16[6,1,64,128]{3,2,1,0:T(8,128)(2,1)S(1)}, bf16[6,1,64,128]{3,2,1,0:T(8,128)(2,1)S(1)}, u32[]{:S(2)}, u32[]{:S(2)}) %collective-permute-start.7) | collective-permute-done | bytes 98336 | tf_op jit(solution)/shard_map/ppermute | solution.py:21
  52.8 0.7 select_maximum_fusion
  59.7 0.7 copy-done.4
  74.8 3.4 %collective-permute-start.8 = (bf16[1,6,64,128]{3,2,1,0:T(8,128)(2,1)S(1)}, bf16[1,6,64,128]{3,2,1,0:T(8,128)(2,1)S(1)}, u32[]{:S(2)}, u32[]{:S(2)}) collective-permute-start(bf16[1,6,64,128]{3,2,1,0:T(8,128)(2,1)S(1)} %get-tuple-element.57), channel_id=1, source_target_pairs={{0,4},{4,8},{8,12},{1,5},{5,9},{9,13},{2,6},{6,10},{10,14},{3,7},{... | collective-permute-start | bytes 294920 | tf_op jit(solution)/shard_map/ppermute | solution.py:31
  78.2 1.3 collective-permute-start.9
  81.5 0.8 collective-permute-done.9
  82.4 3.5 %collective-permute-start.10 = (bf16[4,1,64,128]{3,2,1,0:T(8,128)(2,1)S(1)}, bf16[4,1,64,128]{3,2,1,0:T(8,128)(2,1)S(1)}, u32[]{:S(2)}, u32[]{:S(2)}) collective-permute-start(bf16[4,1,64,128]{3,2,1,0:T(8,128)(2,1)S(1)} %get-tuple-element.61), channel_id=1, source_target_pairs={{0,1},{1,2},{2,3},{4,5},{5,6},{6,7},{8,9},{9,10},{10,11},{12,13},{... | collective-permute-start | bytes 196616 | tf_op jit(solution)/shard_map/ppermute | solution.py:31
  85.9 0.9 pad_maximum_fusion.1
  86.9 1.3 collective-permute-start.11
  88.2 4.8 %collective-permute-done.11 = bf16[4,1,64,128]{3,2,1,0:T(8,128)(2,1)S(1)} collective-permute-done((bf16[4,1,64,128]{3,2,1,0:T(8,128)(2,1)S(1)}, bf16[4,1,64,128]{3,2,1,0:T(8,128)(2,1)S(1)}, u32[]{:S(2)}, u32[]{:S(2)}) %collective-permute-start.11) | collective-permute-done | bytes 65568 | tf_op jit(solution)/shard_map/ppermute | solution.py:31
  100.3 1.0 pad_maximum_fusion
  101.3 0.8 copy.43
  102.1 95.4 %all-reduce.7.cloned.1.call-done = (f32[3,3,3,58,64]{4,3,2,1,0:T(8,128)}, f32[3,3,3,64,53]{3,4,2,1,0:T(8,128)}) async-done(((f32[3,3,3,58,64]{4,3,2,1,0:T(8,128)}, f32[3,3,3,64,53]{3,4,2,1,0:T(8,128)}), (f32[3,3,3,58,64]{4,3,2,1,0:T(8,128)}, f32[3,3,3,64,53]{3,4,2,1,0:T(8,128)})) %all-reduce.7.cloned.1.call-update) | async-done | bytes 767248 | tf_op jit(solution)/shard_map/psum | solution.py:157
  197.5 2.2 %copy.200 = f32[3,3,3,58,64]{4,3,2,1,0:T(8,128)} copy(f32[3,3,3,58,64]{4,3,2,1,0:T(8,128)} %get-tuple-element.95) | data formatting | bytes 801792
  199.7 0.9 copy.201
  (184 shorter events, 37.3 us)
Async XLA Ops:
  7.2 13.5 %copy-start.3 = (bf16[3,3,3,58,64]{4,3,2,1,0:T(8,128)(2,1)S(1)}, bf16[3,3,3,58,64]{4,3,2,1,0:T(8,128)(2,1)}, u32[]{:S(2)}) copy-start(bf16[3,3,3,58,64]{4,3,2,1,0:T(8,128)(2,1)} %param.14) | copy-start | bytes 601348
  7.2 190.3 %all-reduce.7.cloned.1.call-start = ((), (), s32[]{:S(2)}) async-start(), calls=%async_computation | async-start | bytes 3317760 | tf_op jit(solution)/shard_map/psum | solution.py:157
  8.2 3.7 %collective-permute-start = (bf16[1,4,58,128]{3,2,1,0:T(8,128)(2,1)S(1)}, bf16[1,4,58,128]{3,2,1,0:T(8,128)(2,1)S(1)}, u32[]{:S(2)}, u32[]{:S(2)}) collective-permute-start(bf16[1,4,58,128]{3,2,1,0:T(8,128)(2,1)S(1)} %copy.188), channel_id=1, source_target_pairs={{0,4},{4,8},{8,12},{1,5},{5,9},{9,13},{2,6},{6,10},{10,14},{3,7},{... | collective-permute-start | bytes 178184 | tf_op jit(solution)/shard_map/ppermute | solution.py:19
  10.6 5.3 %collective-permute-start.1 = (bf16[1,4,58,128]{3,2,1,0:T(8,128)(2,1)S(1)}, bf16[1,4,58,128]{3,2,1,0:T(8,128)(2,1)S(1)}, u32[]{:S(2)}, u32[]{:S(2)}) collective-permute-start(bf16[1,4,58,128]{3,2,1,0:T(8,128)(2,1)S(1)} %copy.189), channel_id=1, source_target_pairs={{4,0},{8,4},{12,8},{5,1},{9,5},{13,9},{6,2},{10,6},{14,10},{7,3},{... | collective-permute-start | bytes 178184 | tf_op jit(solution)/shard_map/ppermute | solution.py:21
  15.9 5.7 %collective-permute-start.2 = (bf16[6,1,58,128]{3,2,1,0:T(8,128)(2,1)S(1)}, bf16[6,1,58,128]{3,2,1,0:T(8,128)(2,1)S(1)}, u32[]{:S(2)}, u32[]{:S(2)}) collective-permute-start(bf16[6,1,58,128]{3,2,1,0:T(8,128)(2,1)S(1)} %get-tuple-element.64), channel_id=1, source_target_pairs={{0,1},{1,2},{2,3},{4,5},{5,6},{6,7},{8,9},{9,10},{10,11},{12,13},{... | collective-permute-start | bytes 267272 | tf_op jit(solution)/shard_map/ppermute | solution.py:19
  19.4 6.5 %collective-permute-start.3 = (bf16[6,1,58,128]{3,2,1,0:T(8,128)(2,1)S(1)}, bf16[6,1,58,128]{3,2,1,0:T(8,128)(2,1)S(1)}, u32[]{:S(2)}, u32[]{:S(2)}) collective-permute-start(bf16[6,1,58,128]{3,2,1,0:T(8,128)(2,1)S(1)} %get-tuple-element.65), channel_id=1, source_target_pairs={{1,0},{2,1},{3,2},{5,4},{6,5},{7,6},{9,8},{10,9},{11,10},{13,12},{... | collective-permute-start | bytes 267272 | tf_op jit(solution)/shard_map/ppermute | solution.py:21
  31.7 0.9 copy-start
  35.2 4.9 %collective-permute-start.4 = (bf16[1,4,64,128]{3,2,1,0:T(8,128)(2,1)S(1)}, bf16[1,4,64,128]{3,2,1,0:T(8,128)(2,1)S(1)}, u32[]{:S(2)}, u32[]{:S(2)}) collective-permute-start(bf16[1,4,64,128]{3,2,1,0:T(8,128)(2,1)S(1)} %get-tuple-element.66), channel_id=1, source_target_pairs={{0,4},{4,8},{8,12},{1,5},{5,9},{9,13},{2,6},{6,10},{10,14},{3,7},{... | collective-permute-start | bytes 196616 | tf_op jit(solution)/shard_map/ppermute | solution.py:19
  38.6 14.9 %copy-start.1 = (bf16[3,3,3,64,53]{3,4,2,1,0:T(8,128)(2,1)S(1)}, bf16[3,3,3,64,53]{3,4,2,1,0:T(8,128)(2,1)}, u32[]{:S(2)}) copy-start(bf16[3,3,3,64,53]{3,4,2,1,0:T(8,128)(2,1)} %param.15) | copy-start | bytes 549508
  38.6 4.2 %collective-permute-start.5 = (bf16[1,4,64,128]{3,2,1,0:T(8,128)(2,1)S(1)}, bf16[1,4,64,128]{3,2,1,0:T(8,128)(2,1)S(1)}, u32[]{:S(2)}, u32[]{:S(2)}) collective-permute-start(bf16[1,4,64,128]{3,2,1,0:T(8,128)(2,1)S(1)} %get-tuple-element.67), channel_id=1, source_target_pairs={{4,0},{8,4},{12,8},{5,1},{9,5},{13,9},{6,2},{10,6},{14,10},{7,3},{... | collective-permute-start | bytes 196616 | tf_op jit(solution)/shard_map/ppermute | solution.py:21
  42.8 5.7 %collective-permute-start.6 = (bf16[6,1,64,128]{3,2,1,0:T(8,128)(2,1)S(1)}, bf16[6,1,64,128]{3,2,1,0:T(8,128)(2,1)S(1)}, u32[]{:S(2)}, u32[]{:S(2)}) collective-permute-start(bf16[6,1,64,128]{3,2,1,0:T(8,128)(2,1)S(1)} %get-tuple-element.62), channel_id=1, source_target_pairs={{0,1},{1,2},{2,3},{4,5},{5,6},{6,7},{8,9},{9,10},{10,11},{12,13},{... | collective-permute-start | bytes 294920 | tf_op jit(solution)/shard_map/ppermute | solution.py:19
  46.3 6.5 %collective-permute-start.7 = (bf16[6,1,64,128]{3,2,1,0:T(8,128)(2,1)S(1)}, bf16[6,1,64,128]{3,2,1,0:T(8,128)(2,1)S(1)}, u32[]{:S(2)}, u32[]{:S(2)}) collective-permute-start(bf16[6,1,64,128]{3,2,1,0:T(8,128)(2,1)S(1)} %get-tuple-element.63), channel_id=1, source_target_pairs={{1,0},{2,1},{3,2},{5,4},{6,5},{7,6},{9,8},{10,9},{11,10},{13,12},{... | collective-permute-start | bytes 294920 | tf_op jit(solution)/shard_map/ppermute | solution.py:21
  59.5 0.9 copy-start.4
  74.8 6.7 %collective-permute-start.8 = (bf16[1,6,64,128]{3,2,1,0:T(8,128)(2,1)S(1)}, bf16[1,6,64,128]{3,2,1,0:T(8,128)(2,1)S(1)}, u32[]{:S(2)}, u32[]{:S(2)}) collective-permute-start(bf16[1,6,64,128]{3,2,1,0:T(8,128)(2,1)S(1)} %get-tuple-element.57), channel_id=1, source_target_pairs={{0,4},{4,8},{8,12},{1,5},{5,9},{9,13},{2,6},{6,10},{10,14},{3,7},{... | collective-permute-start | bytes 294920 | tf_op jit(solution)/shard_map/ppermute | solution.py:31
  78.2 4.1 %collective-permute-start.9 = (bf16[1,6,64,128]{3,2,1,0:T(8,128)(2,1)S(1)}, bf16[1,6,64,128]{3,2,1,0:T(8,128)(2,1)S(1)}, u32[]{:S(2)}, u32[]{:S(2)}) collective-permute-start(bf16[1,6,64,128]{3,2,1,0:T(8,128)(2,1)S(1)} %get-tuple-element.56), channel_id=1, source_target_pairs={{4,0},{8,4},{12,8},{5,1},{9,5},{13,9},{6,2},{10,6},{14,10},{7,3},{... | collective-permute-start | bytes 294920 | tf_op jit(solution)/shard_map/ppermute | solution.py:31
  82.4 5.8 %collective-permute-start.10 = (bf16[4,1,64,128]{3,2,1,0:T(8,128)(2,1)S(1)}, bf16[4,1,64,128]{3,2,1,0:T(8,128)(2,1)S(1)}, u32[]{:S(2)}, u32[]{:S(2)}) collective-permute-start(bf16[4,1,64,128]{3,2,1,0:T(8,128)(2,1)S(1)} %get-tuple-element.61), channel_id=1, source_target_pairs={{0,1},{1,2},{2,3},{4,5},{5,6},{6,7},{8,9},{9,10},{10,11},{12,13},{... | collective-permute-start | bytes 196616 | tf_op jit(solution)/shard_map/ppermute | solution.py:31
  86.9 6.2 %collective-permute-start.11 = (bf16[4,1,64,128]{3,2,1,0:T(8,128)(2,1)S(1)}, bf16[4,1,64,128]{3,2,1,0:T(8,128)(2,1)S(1)}, u32[]{:S(2)}, u32[]{:S(2)}) collective-permute-start(bf16[4,1,64,128]{3,2,1,0:T(8,128)(2,1)S(1)} %get-tuple-element.60), channel_id=1, source_target_pairs={{1,0},{2,1},{3,2},{5,4},{6,5},{7,6},{9,8},{10,9},{11,10},{13,12},{... | collective-permute-start | bytes 196616 | tf_op jit(solution)/shard_map/ppermute | solution.py:31
  197.5 2.3 %copy-start.2 = (f32[3,3,3,64,53]{3,4,2,1,0:T(8,128)S(1)}, f32[3,3,3,64,53]{3,4,2,1,0:T(8,128)}, u32[]{:S(2)}) copy-start(f32[3,3,3,64,53]{3,4,2,1,0:T(8,128)} %get-tuple-element.96) | copy-start | bytes 1099012
Sparse Core Ops, SparseCore 0:
  101.4 95.9 all-reduce.6
where the time goes:
time: 208 us; the launch traced here: 207 us
  waiting for transfers between devices  116 us (56%)
  matrix products  36.2 us (17%)
  starting transfers between devices  27.7 us (13%)
  between operations  15.4 us (7%)
  local copies, waits for them, and re-layouts  7.62 us (4%)
  other arithmetic  4.08 us (2%)
    psum x1, waiting for transfers between devices, on_device(): grad_first, grad_second = lax.psum((grad_first, grad_second), ('gx', 'gy'))  95.4 us
    dot_general x54, matrix products, correlate(): jnp.einsum('xycz,co->xyoz', window, kernel[step_a, step_b, step_c], prefe...  14.4 us
    ppermute x4, waiting for transfers between devices, extended(): lax.ppermute(head, axis, [((i + 1) % count, i) for i in range(ends)])  14.1 us
    ppermute x4, starting transfers between devices, extended(): lax.ppermute(tail, axis, [(i, (i + 1) % count) for i in range(ends)])  12.7 us
    dot_general x54, matrix products, filter_grad(): jnp.einsum('xycz,xyoz->co', window, slope_term, preferred_element_type=jn...  12.7 us
    ppermute x4, starting transfers between devices, shifted(): lax.ppermute(value, axis, [(source, source + steps) for source in range(l...  9.48 us
    dot_general x27, matrix products, correlate_back(): jnp.einsum('xyoz,io->xyiz', window, kernel[step_a, step_b, step_c], prefe...  9.04 us
    unnamed x17, local copies, waits for them, and re-layouts  6.51 us
  transfers between devices with their start and end apart: 13, of which 9 were waited for; matrix products, arithmetic and copies ran while one was open for 2% of the time, Pallas kernels for 0%

commit v1 on v0

--- a/solution.py
+++ b/solution.py
@@ -154,7 +154,7 @@
     back_grad = summed_x[:, 1 : extent_y - 1].at[:, :1].add(from_left).at[:, -1:].add(from_right)
     slope_term = (back_grad * gate_slope(activation)).astype(jnp.bfloat16)
     grad_first = filter_grad(padded_in, slope_term)
-    grad_first, grad_second = lax.psum((grad_first, grad_second), ("gx", "gy"))
+    grad_first, grad_second = lax.psum(lax.psum((grad_first, grad_second), "gy"), "gx")
     return (prediction, grad_first, grad_second)
 
 

time: 208 us -> 230 us (1.11)
  waiting for transfers between devices: 116 us -> 139 us
    psum x1 -> x2, waiting for transfers between devices: 95.4 us -> 118 us  [the longest x1 72.4 us: on_device(): lax.psum((grad_first, grad_second), 'gy')]
  transfers between devices with their start and end apart: 13 -> 14, of which waited for: 9 -> 10; matrix products, arithmetic and copies ran while one was open for 2% -> 2% of each run, Pallas kernels for 0% -> 0%
where the time goes in v1:
time: 230 us
  waiting for transfers between devices  139 us (60%)
  matrix products  36.2 us (16%)
  starting transfers between devices  27.8 us (12%)
  between operations  15.4 us (7%)
  local copies, waits for them, and re-layouts  7.62 us (3%)
  other arithmetic  4.08 us (2%)
    psum x1, waiting for transfers between devices, on_device(): lax.psum((grad_first, grad_second), 'gy')  72.4 us
    psum x1, waiting for transfers between devices, on_device(): lax.psum(lax.psum((grad_first, grad_second), 'gy'), 'gx')  45.3 us
    dot_general x54, matrix products, correlate(): jnp.einsum('xycz,co->xyoz', window, kernel[step_a, step_b, step_c], prefe...  14.4 us
    ppermute x4, waiting for transfers between devices, extended(): lax.ppermute(head, axis, [((i + 1) % count, i) for i in range(ends)])  14.1 us
    ppermute x4, starting transfers between devices, extended(): lax.ppermute(tail, axis, [(i, (i + 1) % count) for i in range(ends)])  12.7 us
    dot_general x54, matrix products, filter_grad(): jnp.einsum('xycz,xyoz->co', window, slope_term, preferred_element_type=jn...  12.7 us
    ppermute x4, starting transfers between devices, shifted(): lax.ppermute(value, axis, [(source, source + steps) for source in range(l...  9.48 us
    dot_general x27, matrix products, correlate_back(): jnp.einsum('xyoz,io->xyiz', window, kernel[step_a, step_b, step_c], prefe...  9.04 us
  transfers between devices with their start and end apart: 14, of which 10 were waited for; matrix products, arithmetic and copies ran while one was open for 2% of the time, Pallas kernels for 0%

profile of v1, /device:TPU:0, one launch (start us, length us, event | category | flops | bytes accessed | tf_op | source)
XLA Modules:
  0.0 229.8 jit_solution(7250990427173325516)
XLA Ops:
  7.2 0.9 fusion.357
  8.2 2.4 %collective-permute-start = (bf16[1,4,58,128]{3,2,1,0:T(8,128)(2,1)S(1)}, bf16[1,4,58,128]{3,2,1,0:T(8,128)(2,1)S(1)}, u32[]{:S(2)}, u32[]{:S(2)}) collective-permute-start(bf16[1,4,58,128]{3,2,1,0:T(8,128)(2,1)S(1)} %copy.188), channel_id=1, source_target_pairs={{0,4},{4,8},{8,12},{1,5},{5,9},{9,13},{2,6},{6,10},{10,14},{3,7},{... | collective-permute-start | bytes 178184 | tf_op jit(solution)/shard_map/ppermute | solution.py:19
  10.6 1.3 collective-permute-start.1
  11.9 1.2 constant_dynamic-update-slice_fusion.6
  13.1 2.8 %collective-permute-done.1 = bf16[1,4,58,128]{3,2,1,0:T(8,128)(2,1)S(1)} collective-permute-done((bf16[1,4,58,128]{3,2,1,0:T(8,128)(2,1)S(1)}, bf16[1,4,58,128]{3,2,1,0:T(8,128)(2,1)S(1)}, u32[]{:S(2)}, u32[]{:S(2)}) %collective-permute-start.1) | collective-permute-done | bytes 59424 | tf_op jit(solution)/shard_map/ppermute | solution.py:21
  15.9 3.5 %collective-permute-start.2 = (bf16[6,1,58,128]{3,2,1,0:T(8,128)(2,1)S(1)}, bf16[6,1,58,128]{3,2,1,0:T(8,128)(2,1)S(1)}, u32[]{:S(2)}, u32[]{:S(2)}) collective-permute-start(bf16[6,1,58,128]{3,2,1,0:T(8,128)(2,1)S(1)} %get-tuple-element.66), channel_id=1, source_target_pairs={{0,1},{1,2},{2,3},{4,5},{5,6},{6,7},{8,9},{9,10},{10,11},{12,13},{... | collective-permute-start | bytes 267272 | tf_op jit(solution)/shard_map/ppermute | solution.py:19
  19.4 1.3 collective-permute-start.3
  21.0 0.6 collective-permute-done.2
  21.6 4.3 %collective-permute-done.3 = bf16[6,1,58,128]{3,2,1,0:T(8,128)(2,1)S(1)} collective-permute-done((bf16[6,1,58,128]{3,2,1,0:T(8,128)(2,1)S(1)}, bf16[6,1,58,128]{3,2,1,0:T(8,128)(2,1)S(1)}, u32[]{:S(2)}, u32[]{:S(2)}) %collective-permute-start.3) | collective-permute-done | bytes 89120 | tf_op jit(solution)/shard_map/ppermute | solution.py:21
  32.0 0.7 copy-done
  35.2 3.4 %collective-permute-start.4 = (bf16[1,4,64,128]{3,2,1,0:T(8,128)(2,1)S(1)}, bf16[1,4,64,128]{3,2,1,0:T(8,128)(2,1)S(1)}, u32[]{:S(2)}, u32[]{:S(2)}) collective-permute-start(bf16[1,4,64,128]{3,2,1,0:T(8,128)(2,1)S(1)} %get-tuple-element.68), channel_id=1, source_target_pairs={{0,4},{4,8},{8,12},{1,5},{5,9},{9,13},{2,6},{6,10},{10,14},{3,7},{... | collective-permute-start | bytes 196616 | tf_op jit(solution)/shard_map/ppermute | solution.py:19
  38.6 1.4 collective-permute-start.5
  40.0 2.7 %collective-permute-done.5 = bf16[1,4,64,128]{3,2,1,0:T(8,128)(2,1)S(1)} collective-permute-done((bf16[1,4,64,128]{3,2,1,0:T(8,128)(2,1)S(1)}, bf16[1,4,64,128]{3,2,1,0:T(8,128)(2,1)S(1)}, u32[]{:S(2)}, u32[]{:S(2)}) %collective-permute-start.5) | collective-permute-done | bytes 65568 | tf_op jit(solution)/shard_map/ppermute | solution.py:21
  42.8 3.5 %collective-permute-start.6 = (bf16[6,1,64,128]{3,2,1,0:T(8,128)(2,1)S(1)}, bf16[6,1,64,128]{3,2,1,0:T(8,128)(2,1)S(1)}, u32[]{:S(2)}, u32[]{:S(2)}) collective-permute-start(bf16[6,1,64,128]{3,2,1,0:T(8,128)(2,1)S(1)} %get-tuple-element.64), channel_id=1, source_target_pairs={{0,1},{1,2},{2,3},{4,5},{5,6},{6,7},{8,9},{9,10},{10,11},{12,13},{... | collective-permute-start | bytes 294920 | tf_op jit(solution)/shard_map/ppermute | solution.py:19
  46.3 1.5 collective-permute-start.7
  47.8 0.7 collective-permute-done.6
  48.5 4.3 %collective-permute-done.7 = bf16[6,1,64,128]{3,2,1,0:T(8,128)(2,1)S(1)} collective-permute-done((bf16[6,1,64,128]{3,2,1,0:T(8,128)(2,1)S(1)}, bf16[6,1,64,128]{3,2,1,0:T(8,128)(2,1)S(1)}, u32[]{:S(2)}, u32[]{:S(2)}) %collective-permute-start.7) | collective-permute-done | bytes 98336 | tf_op jit(solution)/shard_map/ppermute | solution.py:21
  52.8 0.7 select_maximum_fusion
  59.7 0.7 copy-done.4
  74.8 3.4 %collective-permute-start.8 = (bf16[1,6,64,128]{3,2,1,0:T(8,128)(2,1)S(1)}, bf16[1,6,64,128]{3,2,1,0:T(8,128)(2,1)S(1)}, u32[]{:S(2)}, u32[]{:S(2)}) collective-permute-start(bf16[1,6,64,128]{3,2,1,0:T(8,128)(2,1)S(1)} %get-tuple-element.59), channel_id=1, source_target_pairs={{0,4},{4,8},{8,12},{1,5},{5,9},{9,13},{2,6},{6,10},{10,14},{3,7},{... | collective-permute-start | bytes 294920 | tf_op jit(solution)/shard_map/ppermute | solution.py:31
  78.2 1.3 collective-permute-start.9
  81.5 0.8 collective-permute-done.9
  82.4 3.5 %collective-permute-start.10 = (bf16[4,1,64,128]{3,2,1,0:T(8,128)(2,1)S(1)}, bf16[4,1,64,128]{3,2,1,0:T(8,128)(2,1)S(1)}, u32[]{:S(2)}, u32[]{:S(2)}) collective-permute-start(bf16[4,1,64,128]{3,2,1,0:T(8,128)(2,1)S(1)} %get-tuple-element.63), channel_id=1, source_target_pairs={{0,1},{1,2},{2,3},{4,5},{5,6},{6,7},{8,9},{9,10},{10,11},{12,13},{... | collective-permute-start | bytes 196616 | tf_op jit(solution)/shard_map/ppermute | solution.py:31
  85.9 0.9 pad_maximum_fusion.1
  86.9 1.3 collective-permute-start.11
  88.2 4.8 %collective-permute-done.11 = bf16[4,1,64,128]{3,2,1,0:T(8,128)(2,1)S(1)} collective-permute-done((bf16[4,1,64,128]{3,2,1,0:T(8,128)(2,1)S(1)}, bf16[4,1,64,128]{3,2,1,0:T(8,128)(2,1)S(1)}, u32[]{:S(2)}, u32[]{:S(2)}) %collective-permute-start.11) | collective-permute-done | bytes 65568 | tf_op jit(solution)/shard_map/ppermute | solution.py:31
  100.3 1.0 pad_maximum_fusion
  101.3 72.4 %all-reduce.9.cloned.1.call-done = (f32[3,3,3,58,64]{4,3,2,1,0:T(8,128)}, f32[3,3,3,64,53]{3,4,2,1,0:T(8,128)}) async-done(((f32[3,3,3,58,64]{4,3,2,1,0:T(8,128)}, f32[3,3,3,64,53]{3,4,2,1,0:T(8,128)}), (f32[3,3,3,58,64]{4,3,2,1,0:T(8,128)}, f32[3,3,3,64,53]{3,4,2,1,0:T(8,128)})) %all-reduce.9.cloned.1.call-update) | async-done | bytes 767248 | tf_op jit(solution)/shard_map/psum | solution.py:157
  173.8 0.8 copy.43
  174.5 45.3 %all-reduce.11.cloned.1.call-done = (f32[3,3,3,58,64]{4,3,2,1,0:T(8,128)}, f32[3,3,3,64,53]{3,4,2,1,0:T(8,128)}) async-done(((f32[3,3,3,58,64]{4,3,2,1,0:T(8,128)}, f32[3,3,3,64,53]{3,4,2,1,0:T(8,128)}), (f32[3,3,3,58,64]{4,3,2,1,0:T(8,128)}, f32[3,3,3,64,53]{3,4,2,1,0:T(8,128)})) %all-reduce.11.cloned.1.call-update) | async-done | bytes 767248 | tf_op jit(solution)/shard_map/psum | solution.py:157
  219.8 2.2 copy.202
  222.1 0.9 copy.203
  (187 shorter events, 38.0 us)
Async XLA Ops:
  7.2 13.5 %copy-start.3 = (bf16[3,3,3,58,64]{4,3,2,1,0:T(8,128)(2,1)S(1)}, bf16[3,3,3,58,64]{4,3,2,1,0:T(8,128)(2,1)}, u32[]{:S(2)}) copy-start(bf16[3,3,3,58,64]{4,3,2,1,0:T(8,128)(2,1)} %param.14) | copy-start | bytes 601348
  7.2 166.6 %all-reduce.9.cloned.1.call-start = ((), (), s32[]{:S(2)}) async-start(), calls=%async_computation | async-start | bytes 3317760 | tf_op jit(solution)/shard_map/psum | solution.py:157
  8.2 3.7 %collective-permute-start = (bf16[1,4,58,128]{3,2,1,0:T(8,128)(2,1)S(1)}, bf16[1,4,58,128]{3,2,1,0:T(8,128)(2,1)S(1)}, u32[]{:S(2)}, u32[]{:S(2)}) collective-permute-start(bf16[1,4,58,128]{3,2,1,0:T(8,128)(2,1)S(1)} %copy.188), channel_id=1, source_target_pairs={{0,4},{4,8},{8,12},{1,5},{5,9},{9,13},{2,6},{6,10},{10,14},{3,7},{... | collective-permute-start | bytes 178184 | tf_op jit(solution)/shard_map/ppermute | solution.py:19
  10.6 5.3 %collective-permute-start.1 = (bf16[1,4,58,128]{3,2,1,0:T(8,128)(2,1)S(1)}, bf16[1,4,58,128]{3,2,1,0:T(8,128)(2,1)S(1)}, u32[]{:S(2)}, u32[]{:S(2)}) collective-permute-start(bf16[1,4,58,128]{3,2,1,0:T(8,128)(2,1)S(1)} %copy.189), channel_id=1, source_target_pairs={{4,0},{8,4},{12,8},{5,1},{9,5},{13,9},{6,2},{10,6},{14,10},{7,3},{... | collective-permute-start | bytes 178184 | tf_op jit(solution)/shard_map/ppermute | solution.py:21
  15.9 5.7 %collective-permute-start.2 = (bf16[6,1,58,128]{3,2,1,0:T(8,128)(2,1)S(1)}, bf16[6,1,58,128]{3,2,1,0:T(8,128)(2,1)S(1)}, u32[]{:S(2)}, u32[]{:S(2)}) collective-permute-start(bf16[6,1,58,128]{3,2,1,0:T(8,128)(2,1)S(1)} %get-tuple-element.66), channel_id=1, source_target_pairs={{0,1},{1,2},{2,3},{4,5},{5,6},{6,7},{8,9},{9,10},{10,11},{12,13},{... | collective-permute-start | bytes 267272 | tf_op jit(solution)/shard_map/ppermute | solution.py:19
  19.4 6.5 %collective-permute-start.3 = (bf16[6,1,58,128]{3,2,1,0:T(8,128)(2,1)S(1)}, bf16[6,1,58,128]{3,2,1,0:T(8,128)(2,1)S(1)}, u32[]{:S(2)}, u32[]{:S(2)}) collective-permute-start(bf16[6,1,58,128]{3,2,1,0:T(8,128)(2,1)S(1)} %get-tuple-element.67), channel_id=1, source_target_pairs={{1,0},{2,1},{3,2},{5,4},{6,5},{7,6},{9,8},{10,9},{11,10},{13,12},{... | collective-permute-start | bytes 267272 | tf_op jit(solution)/shard_map/ppermute | solution.py:21
  31.7 0.9 copy-start
  35.2 4.9 %collective-permute-start.4 = (bf16[1,4,64,128]{3,2,1,0:T(8,128)(2,1)S(1)}, bf16[1,4,64,128]{3,2,1,0:T(8,128)(2,1)S(1)}, u32[]{:S(2)}, u32[]{:S(2)}) collective-permute-start(bf16[1,4,64,128]{3,2,1,0:T(8,128)(2,1)S(1)} %get-tuple-element.68), channel_id=1, source_target_pairs={{0,4},{4,8},{8,12},{1,5},{5,9},{9,13},{2,6},{6,10},{10,14},{3,7},{... | collective-permute-start | bytes 196616 | tf_op jit(solution)/shard_map/ppermute | solution.py:19
  38.6 14.9 %copy-start.1 = (bf16[3,3,3,64,53]{3,4,2,1,0:T(8,128)(2,1)S(1)}, bf16[3,3,3,64,53]{3,4,2,1,0:T(8,128)(2,1)}, u32[]{:S(2)}) copy-start(bf16[3,3,3,64,53]{3,4,2,1,0:T(8,128)(2,1)} %param.15) | copy-start | bytes 549508
  38.6 4.2 %collective-permute-start.5 = (bf16[1,4,64,128]{3,2,1,0:T(8,128)(2,1)S(1)}, bf16[1,4,64,128]{3,2,1,0:T(8,128)(2,1)S(1)}, u32[]{:S(2)}, u32[]{:S(2)}) collective-permute-start(bf16[1,4,64,128]{3,2,1,0:T(8,128)(2,1)S(1)} %get-tuple-element.69), channel_id=1, source_target_pairs={{4,0},{8,4},{12,8},{5,1},{9,5},{13,9},{6,2},{10,6},{14,10},{7,3},{... | collective-permute-start | bytes 196616 | tf_op jit(solution)/shard_map/ppermute | solution.py:21
  42.8 5.7 %collective-permute-start.6 = (bf16[6,1,64,128]{3,2,1,0:T(8,128)(2,1)S(1)}, bf16[6,1,64,128]{3,2,1,0:T(8,128)(2,1)S(1)}, u32[]{:S(2)}, u32[]{:S(2)}) collective-permute-start(bf16[6,1,64,128]{3,2,1,0:T(8,128)(2,1)S(1)} %get-tuple-element.64), channel_id=1, source_target_pairs={{0,1},{1,2},{2,3},{4,5},{5,6},{6,7},{8,9},{9,10},{10,11},{12,13},{... | collective-permute-start | bytes 294920 | tf_op jit(solution)/shard_map/ppermute | solution.py:19
  46.3 6.5 %collective-permute-start.7 = (bf16[6,1,64,128]{3,2,1,0:T(8,128)(2,1)S(1)}, bf16[6,1,64,128]{3,2,1,0:T(8,128)(2,1)S(1)}, u32[]{:S(2)}, u32[]{:S(2)}) collective-permute-start(bf16[6,1,64,128]{3,2,1,0:T(8,128)(2,1)S(1)} %get-tuple-element.65), channel_id=1, source_target_pairs={{1,0},{2,1},{3,2},{5,4},{6,5},{7,6},{9,8},{10,9},{11,10},{13,12},{... | collective-permute-start | bytes 294920 | tf_op jit(solution)/shard_map/ppermute | solution.py:21
  59.5 0.9 copy-start.4
  74.8 6.7 %collective-permute-start.8 = (bf16[1,6,64,128]{3,2,1,0:T(8,128)(2,1)S(1)}, bf16[1,6,64,128]{3,2,1,0:T(8,128)(2,1)S(1)}, u32[]{:S(2)}, u32[]{:S(2)}) collective-permute-start(bf16[1,6,64,128]{3,2,1,0:T(8,128)(2,1)S(1)} %get-tuple-element.59), channel_id=1, source_target_pairs={{0,4},{4,8},{8,12},{1,5},{5,9},{9,13},{2,6},{6,10},{10,14},{3,7},{... | collective-permute-start | bytes 294920 | tf_op jit(solution)/shard_map/ppermute | solution.py:31
  78.2 4.1 %collective-permute-start.9 = (bf16[1,6,64,128]{3,2,1,0:T(8,128)(2,1)S(1)}, bf16[1,6,64,128]{3,2,1,0:T(8,128)(2,1)S(1)}, u32[]{:S(2)}, u32[]{:S(2)}) collective-permute-start(bf16[1,6,64,128]{3,2,1,0:T(8,128)(2,1)S(1)} %get-tuple-element.58), channel_id=1, source_target_pairs={{4,0},{8,4},{12,8},{5,1},{9,5},{13,9},{6,2},{10,6},{14,10},{7,3},{... | collective-permute-start | bytes 294920 | tf_op jit(solution)/shard_map/ppermute | solution.py:31
  82.4 5.8 %collective-permute-start.10 = (bf16[4,1,64,128]{3,2,1,0:T(8,128)(2,1)S(1)}, bf16[4,1,64,128]{3,2,1,0:T(8,128)(2,1)S(1)}, u32[]{:S(2)}, u32[]{:S(2)}) collective-permute-start(bf16[4,1,64,128]{3,2,1,0:T(8,128)(2,1)S(1)} %get-tuple-element.63), channel_id=1, source_target_pairs={{0,1},{1,2},{2,3},{4,5},{5,6},{6,7},{8,9},{9,10},{10,11},{12,13},{... | collective-permute-start | bytes 196616 | tf_op jit(solution)/shard_map/ppermute | solution.py:31
  86.9 6.2 %collective-permute-start.11 = (bf16[4,1,64,128]{3,2,1,0:T(8,128)(2,1)S(1)}, bf16[4,1,64,128]{3,2,1,0:T(8,128)(2,1)S(1)}, u32[]{:S(2)}, u32[]{:S(2)}) collective-permute-start(bf16[4,1,64,128]{3,2,1,0:T(8,128)(2,1)S(1)} %get-tuple-element.62), channel_id=1, source_target_pairs={{1,0},{2,1},{3,2},{5,4},{6,5},{7,6},{9,8},{10,9},{11,10},{13,12},{... | collective-permute-start | bytes 196616 | tf_op jit(solution)/shard_map/ppermute | solution.py:31
  101.3 118.5 %all-reduce.11.cloned.1.call-start = ((), (), s32[]{:S(2)}) async-start(), calls=%async_computation.1 | async-start | bytes 3317760 | tf_op jit(solution)/shard_map/psum | solution.py:157
  219.8 2.3 copy-start.2
Sparse Core Ops, SparseCore 0:
  101.4 72.2 all-reduce.8
  176.2 43.5 all-reduce.10
